TPU v7x, 32 devices: a whole 2x2x4 slice. The times are simulated.
32 devices in a mesh: parts: 2 (over y), ctx: 4 (over z), wt: 2 (over x), sub: 2 (over core).
Axes of the slice: x: 2, y: 2, z: 4, core: 2. Of those that a mesh axis runs over, the one named last changes fastest.
Arguments:
- tokens: bfloat16 [2048, 4096], P(('parts', 'ctx', 'wt')), parts along dimension 0, may hold values from -6 to 6
- block_order: int32 [32], P('parts'), parts along dimension 0, may hold values from 0 to 15, each once
- q_weight: bfloat16 [4096, 2048], P('wt', 'sub')
- key_value_weight: bfloat16 [4096, 4, 2, 128], P('wt', 'sub'), may hold values from -0.09375 to 0.09375
- out_weight: bfloat16 [2048, 4096], P('sub', 'wt'), may hold values from -0.5 to 0.5
Outputs:
- attended: bfloat16 [2048, 4096], P(('parts', 'ctx', 'wt'), 'sub'), parts along dimension 0
There are 2 independent parts, one for each index of `parts`. A program takes and returns all parts, laid end to end along the dimension named above; an argument that names none is the same for every part. Nothing has to cross between parts.
Inputs may be any that keep to these rules, and one draw needn't show every extreme that they name: block_order is a permutation of the 16 block numbers.
All inputs are finite; a program needn't handle non-finite values.
Results may differ from a plain program's by a relative error of at most 0.014.
The roundings to bfloat16 on the way count: a program that leaves them out, or rounds other values in their place, can miss the bound.
Values may be sent and summed in bfloat16 or wider, within the bound.
A program may use at most 128 MiB of HBM per device.

v0:
```python
import jax
import jax.numpy as jnp
from jax import lax
from jax.sharding import PartitionSpec as P

rope_base = 500000.0
epsilon = 1e-05


def token_positions(row_ids, block_order, block_len):
    number = block_order.shape[0]
    blocks = row_ids // block_len
    equal = blocks[:, None] == jnp.arange(number, dtype=jnp.int32)[None, :]
    chosen = jnp.sum(jnp.where(equal, block_order[None, :], 0), axis=1)
    return chosen * block_len + row_ids % block_len


def rotary(values_in, positions, head_dim):
    half_dim = head_dim // 2
    inverse_freq = rope_base ** (-(jnp.arange(half_dim, dtype=jnp.float32) * 2.0 / head_dim))
    angles = positions.astype(jnp.float32)[:, None] * inverse_freq[None, :]
    cosine = jnp.concatenate([jnp.cos(angles), jnp.cos(angles)], axis=1)[:, None, :]
    sine = jnp.concatenate([jnp.sin(angles), jnp.sin(angles)], axis=1)[:, None, :]
    rotated = jnp.concatenate([-values_in[..., half_dim:], values_in[..., :half_dim]], axis=-1)
    return values_in * cosine + rotated * sine


def body(tokens, block_order, q_weight, key_value_weight, out_weight):
    tok_rows = tokens.shape[0]
    block_len = tok_rows // 2
    head_dim = key_value_weight.shape[3]
    kv_local = key_value_weight.shape[1]
    q_cols = q_weight.shape[1]
    q_local = q_cols // head_dim
    group = q_local // kv_local
    kv_cols = kv_local * 2 * head_dim
    kv_flat = key_value_weight.reshape(key_value_weight.shape[0], kv_cols)
    own_first = lax.axis_index(("ctx", "wt")) * tok_rows
    own_ids = own_first + jnp.arange(tok_rows, dtype=jnp.int32)
    own_positions = token_positions(own_ids, block_order, block_len)
    widened = tokens.astype(jnp.float32)
    normalized_input = (
        widened * lax.rsqrt(jnp.mean(widened * widened, axis=1, keepdims=True) + epsilon)
    ).astype(jnp.bfloat16)
    queries = jnp.dot(
        normalized_input,
        lax.all_gather(q_weight, "wt", axis=0, tiled=True),
        preferred_element_type=jnp.float32,
    )
    key_value_rows = jnp.dot(
        normalized_input,
        lax.all_gather(kv_flat, "wt", axis=0, tiled=True),
        preferred_element_type=jnp.float32,
    )
    queries = queries.reshape(tok_rows, q_local, head_dim)
    key_value_rows = key_value_rows.reshape(tok_rows, kv_local, 2, head_dim)
    q_rot = rotary(queries, own_positions, head_dim).astype(jnp.bfloat16)
    k_rot = rotary(key_value_rows[:, :, 0, :], own_positions, head_dim).astype(jnp.bfloat16)
    value_rows = key_value_rows[:, :, 1, :].astype(jnp.bfloat16)
    q_grouped = jnp.transpose(q_rot.reshape(tok_rows, kv_local, group, head_dim), (1, 2, 0, 3))
    q_grouped = q_grouped.reshape(kv_local, group * tok_rows, head_dim)
    query_positions = jnp.tile(own_positions, group)
    score_factor = 1.0 / head_dim**0.5
    key_part = lax.all_gather(k_rot, ("ctx", "wt"), axis=0, tiled=True)
    value_part = lax.all_gather(value_rows, ("ctx", "wt"), axis=0, tiled=True)
    count = key_part.shape[0]
    key_ids = jnp.arange(count, dtype=jnp.int32)
    key_positions = token_positions(key_ids, block_order, block_len)
    visible = query_positions[:, None] >= key_positions[None, :]
    old_max = jnp.full((kv_local, group * tok_rows), -1e30, jnp.float32)
    scores = (
        jnp.einsum("hqd,khd->hqk", q_grouped, key_part, preferred_element_type=jnp.float32)
        * score_factor
    )
    scores = jnp.where(visible[None], scores, -1e30)
    new_max = jnp.maximum(old_max, jnp.max(scores, axis=2))
    weights = jnp.where(visible[None], jnp.exp(scores - new_max[..., None]), 0.0)
    new_total = jnp.sum(weights, axis=2)
    new_acc = jnp.einsum(
        "hqk,khd->hqd", weights.astype(jnp.bfloat16), value_part, preferred_element_type=jnp.float32
    )
    heads_out = new_acc / new_total[..., None]
    heads_out = jnp.transpose(heads_out.reshape(kv_local, group, tok_rows, head_dim), (2, 0, 1, 3))
    heads_out = heads_out.reshape(tok_rows, q_cols).astype(jnp.bfloat16)
    partial_out = jnp.dot(
        heads_out,
        lax.all_gather(out_weight, "wt", axis=1, tiled=True),
        preferred_element_type=jnp.float32,
    )
    return lax.psum_scatter(
        partial_out.astype(jnp.bfloat16), "sub", scatter_dimension=1, tiled=True
    )


def solution(mesh):
    in_specs = (
        P(("parts", "ctx", "wt"), None),
        P("parts"),
        P("wt", "sub"),
        P("wt", "sub", None, None),
        P("sub", "wt"),
    )
    out_specs = P(("parts", "ctx", "wt"), "sub")
    return jax.shard_map(body, mesh=mesh, in_specs=in_specs, out_specs=out_specs, check_vma=False)
```

profile of v0, /device:TPU:0, one launch (start us, length us, event | category | flops | bytes accessed | tf_op | source)
XLA Modules:
  0.0 318.9 jit_solution(17308050258334250507)
XLA Ops:
  6.5 0.0 all-gather.7.cloned.1.call-start
  6.5 4.1 %reshape.158 = bf16[2048,512]{1,0:T(8,128)(2,1)} reshape(bf16[2048,2,2,128]{3,2,1,0:T(2,128)(2,1)} %param.8) | data formatting | bytes 4194304 | tf_op jit(solution)/shard_map/reshape | solution.py:37
  10.6 0.0 all-gather.7.cloned.1.call-update
  10.7 0.0 copy-start.1
  10.7 0.0 copy-start
  10.7 0.0 all-gather.5.cloned.1.call-start
  10.7 0.7 all-gather.5.cloned.1.call-update
  11.4 0.0 all-gather.9.cloned.1.call-start
  11.5 0.7 all-gather.9.cloned.1.call-update
  12.2 0.0 reduce-scatter.2.cloned.1.call-start
  12.3 0.0 copy-done.1
  12.3 0.1 select_reduce_fusion.1
  12.4 0.1 select_reduce_fusion
  12.5 0.3 multiply_cosine_fusion
  12.8 0.1 pad_maximum_fusion
  12.9 0.0 copy-done
  12.9 0.3 fusion.3
  13.2 0.4 broadcast_compare_fusion
  13.6 56.7 %all-gather.7.cloned.1.call-done = bf16[4096,512]{1,0:T(8,128)(2,1)} async-done(((bf16[2048,512]{1,0:T(8,128)(2,1)}), bf16[4096,512]{1,0:T(8,128)(2,1)}) %all-gather.7.cloned.1.call-update) | async-done | bytes 4194320 | tf_op jit(solution)/shard_map/all_gather | solution.py:52
  70.3 2.9 fusion.17
  73.2 0.2 reshape.159
  73.4 0.1 slice.27
  73.5 0.1 slice.30
  73.7 0.1 slice_negate_fusion.1
  73.8 0.1 fusion.23
  73.9 31.9 %all_gather.17 = bf16[1024,2,128]{2,0,1:T(8,128)(2,1)S(1)} all-gather(bf16[128,2,128]{2,0,1:T(8,128)(2,1)S(1)} %fusion.23), channel_id=1, replica_groups=mesh['parts'=2,'ctx'=4,'wt'=2,'sub'=2] {'ctx','wt'}, dimensions={0}, use_global_device_ids=true | all-gather | bytes 589824 | tf_op jit(solution)/shard_map/all_gather | solution.py:64
  105.8 31.8 %all-gather = bf16[1024,2,1,128]{3,0,1,2:T(8,128)(2,1)S(1)} all-gather(bf16[128,2,1,128]{3,0,1,2:T(8,128)(2,1)S(1)} %copy.24), channel_id=2, replica_groups=mesh['parts'=2,'ctx'=4,'wt'=2,'sub'=2] {'ctx','wt'}, dimensions={0}, use_global_device_ids=true | all-gather | bytes 589824 | tf_op jit(solution)/shard_map/all_gather | solution.py:65
  137.6 55.1 %all-gather.5.cloned.1.call-done = bf16[4096,1024]{1,0:T(8,128)(2,1)} async-done(((bf16[2048,1024]{1,0:T(8,128)(2,1)}), bf16[4096,1024]{1,0:T(8,128)(2,1)}) %all-gather.5.cloned.1.call-update) | async-done | bytes 8388624 | tf_op jit(solution)/shard_map/all_gather | solution.py:47
  192.7 4.7 %fusion.19 = f32[128,1024]{1,0:T(8,128)S(1)} fusion(bf16[4096,1024]{1,0:T(8,128)(2,1)} %all-gather.5.cloned.1.call-done, bf16[128,4096]{1,0:T(8,128)(2,1)S(1)} %copy-done, f32[128]{0:T(128)S(1)} %add_rsqrt_fusion), kind=kOutput, calls=%fused_computation.21 | convolution fusion | flops 1075314688 | bytes 9961984 | tf_op jit(solution)/shard_map/dot_general | solution.py:45
  197.4 0.2 reshape.155
  197.6 0.1 copy.19
  197.7 0.2 slice_negate_fusion
  197.9 0.4 fusion.21
  198.4 1.1 fusion
  199.5 1.5 fusion.1
  200.9 1.6 fusion.11
  202.5 0.2 copy.16
  202.7 95.2 %all-gather.9.cloned.1.call-done = bf16[1024,4096]{1,0:T(8,128)(2,1)} async-done(((bf16[1024,2048]{1,0:T(8,128)(2,1)}), bf16[1024,4096]{1,0:T(8,128)(2,1)}) %all-gather.9.cloned.1.call-update) | async-done | bytes 8388624 | tf_op jit(solution)/shard_map/all_gather | solution.py:87
  297.9 5.7 %convolution_convert_fusion = bf16[128,4096]{1,0:T(8,128)(2,1)} fusion(bf16[128,1024]{0,1:T(8,128)(2,1)S(1)} %bitcast.31, bf16[1024,4096]{1,0:T(8,128)(2,1)} %all-gather.9.cloned.1.call-done), kind=kOutput, calls=%fused_computation | convolution fusion | flops 1074266112 | bytes 9699328 | tf_op jit(solution)/shard_map/dot_general | solution.py:85
  303.7 0.0 reduce-scatter.2.cloned.1.call-update
  303.7 8.7 %reduce-scatter.2.cloned.1.call-done = bf16[128,2048]{1,0:T(8,128)(2,1)} async-done(((bf16[128,4096]{1,0:T(8,128)(2,1)}), bf16[128,2048]{1,0:T(8,128)(2,1)}) %reduce-scatter.2.cloned.1.call-update) | async-done | bytes 524304 | tf_op jit(solution)/shard_map/reduce_scatter | solution.py:90
  (11 shorter events, 0.1 us)
Async XLA Ops:
  6.5 63.7 %all-gather.7.cloned.1.call-start = ((), (), s32[]{:S(2)}) async-start(), calls=%async_computation.2 | async-start | bytes 6291456 | tf_op jit(solution)/shard_map/all_gather | solution.py:52
  10.7 1.6 copy-start.1
  10.7 2.2 copy-start
  10.7 182.0 %all-gather.5.cloned.1.call-start = ((), (), s32[]{:S(2)}) async-start(), calls=%async_computation.1 | async-start | bytes 12582912 | tf_op jit(solution)/shard_map/all_gather | solution.py:47
  11.4 286.5 %all-gather.9.cloned.1.call-start = ((), (), s32[]{:S(2)}) async-start(), calls=%async_computation.3 | async-start | bytes 12582912 | tf_op jit(solution)/shard_map/all_gather | solution.py:87
  12.2 300.2 %reduce-scatter.2.cloned.1.call-start = ((), (), s32[]{:S(2)}) async-start(), calls=%async_computation.4 | async-start | bytes 1572864 | tf_op jit(solution)/shard_map/reduce_scatter | solution.py:90
Sparse Core Ops, SparseCore 0:
  10.8 59.4 all-gather.6
  71.8 120.8 all-gather.4
  194.3 103.6 all-gather.8
  303.8 8.5 reduce-scatter.1
where the time goes:
time: 319 us
  waiting for transfers between devices  217 us (68%)
  blocking collectives  63.7 us (20%)
  matrix products  16 us (5%)
  between operations  13.3 us (4%)
  local copies, waits for them, and re-layouts  5.11 us (2%)
  other arithmetic  3.58 us (1%)
    all_gather x1, waiting for transfers between devices, body(): lax.all_gather(out_weight, 'wt', axis=1, tiled=True)  95.2 us
    all_gather x1, waiting for transfers between devices, body(): lax.all_gather(kv_flat, 'wt', axis=0, tiled=True)  56.7 us
    all_gather x1, waiting for transfers between devices, body(): lax.all_gather(q_weight, 'wt', axis=0, tiled=True)  55.1 us
    all_gather x1, blocking collectives, body(): key_part = lax.all_gather(k_rot, ('ctx', 'wt'), axis=0, tiled=True)  31.9 us
    all_gather x1, blocking collectives, body(): value_part = lax.all_gather(value_rows, ('ctx', 'wt'), axis=0, tiled=True)  31.8 us
    reduce_scatter x1, waiting for transfers between devices, body(): lax.psum_scatter(partial_out.astype(jnp.bfloat16), 'sub', scatter_dimensi...  8.72 us
  transfers between devices with their start and end apart: 4, of which 4 were waited for; matrix products, arithmetic and copies ran while one was open for 5% of the time, Pallas kernels for 0%

commit v1 on v0

--- a/solution.py
+++ b/solution.py
@@ -61,8 +61,13 @@
     q_grouped = q_grouped.reshape(kv_local, group * tok_rows, head_dim)
     query_positions = jnp.tile(own_positions, group)
     score_factor = 1.0 / head_dim**0.5
-    key_part = lax.all_gather(k_rot, ("ctx", "wt"), axis=0, tiled=True)
-    value_part = lax.all_gather(value_rows, ("ctx", "wt"), axis=0, tiled=True)
+    key_part, value_part = jnp.split(
+        lax.all_gather(
+            jnp.concatenate([k_rot, value_rows], axis=1), ("ctx", "wt"), axis=0, tiled=True
+        ),
+        [k_rot.shape[1]],
+        1,
+    )
     count = key_part.shape[0]
     key_ids = jnp.arange(count, dtype=jnp.int32)
     key_positions = token_positions(key_ids, block_order, block_len)

time: 319 us -> 344 us (1.078)
  waiting for transfers between devices: 217 us -> 304 us
  blocking collectives: 63.7 us -> 0 us
    all_gather x2 -> x0, blocking collectives: 63.7 us -> none  [the longest x1 31.9 us: body(): key_part = lax.all_gather(k_rot, ('ctx', 'wt'), axis=0, tiled=True)]
    all_gather x1, waiting for transfers between devices: 55.1 us -> 100 us  [body(): lax.all_gather(q_weight, 'wt', axis=0, tiled=True)]
    all_gather x0 -> x1, waiting for transfers between devices: none -> 36.7 us  [body(): lax.all_gather(jnp.concatenate([k_rot, value_rows], axis=1), ('ctx', 'wt'...]
    all_gather x1, waiting for transfers between devices: 95.2 us -> 99.3 us  [body(): lax.all_gather(out_weight, 'wt', axis=1, tiled=True)]
  transfers between devices with their start and end apart: 4 -> 5, of which waited for: 4 -> 5; matrix products, arithmetic and copies ran while one was open for 5% -> 5% of each run, Pallas kernels for 0% -> 0%
where the time goes in v1:
time: 344 us; the launch traced here: 343 us
  waiting for transfers between devices  304 us (88%)
  matrix products  16.5 us (5%)
  between operations  13.3 us (4%)
  local copies, waits for them, and re-layouts  5.11 us (1%)
  other arithmetic  4.25 us (1%)
    all_gather x1, waiting for transfers between devices, body(): lax.all_gather(q_weight, 'wt', axis=0, tiled=True)  100 us
    all_gather x1, waiting for transfers between devices, body(): lax.all_gather(out_weight, 'wt', axis=1, tiled=True)  99.3 us
    all_gather x1, waiting for transfers between devices, body(): lax.all_gather(kv_flat, 'wt', axis=0, tiled=True)  57.9 us
    all_gather x1, waiting for transfers between devices, body(): lax.all_gather(jnp.concatenate([k_rot, value_rows], axis=1), ('ctx', 'wt'...  36.7 us
    reduce_scatter x1, waiting for transfers between devices, body(): lax.psum_scatter(partial_out.astype(jnp.bfloat16), 'sub', scatter_dimensi...  8.72 us
  transfers between devices with their start and end apart: 5, of which 5 were waited for; matrix products, arithmetic and copies ran while one was open for 5% of the time, Pallas kernels for 0%

profile of v1, /device:TPU:0, one launch (start us, length us, event | category | flops | bytes accessed | tf_op | source)
XLA Modules:
  0.0 343.4 jit_solution(928204523938229370)
XLA Ops:
  6.5 0.0 all-gather.7.cloned.1.call-start
  6.5 4.1 %reshape.158 = bf16[2048,512]{1,0:T(8,128)(2,1)} reshape(bf16[2048,2,2,128]{3,2,1,0:T(2,128)(2,1)} %param.8) | data formatting | bytes 4194304 | tf_op jit(solution)/shard_map/reshape | solution.py:37
  10.6 0.0 copy-start.1
  10.6 0.0 copy-start
  10.6 0.0 all-gather.7.cloned.1.call-update
  10.7 0.0 all-gather.5.cloned.1.call-start
  10.7 0.7 all-gather.5.cloned.1.call-update
  11.4 0.0 all-gather.9.cloned.1.call-start
  11.5 0.0 copy-done.1
  11.5 0.1 select_reduce_fusion.1
  11.6 0.3 multiply_cosine_fusion
  11.9 0.1 pad_maximum_fusion.1
  12.0 0.0 copy-done
  12.1 0.3 fusion.3
  12.4 57.9 %all-gather.7.cloned.1.call-done = bf16[4096,512]{1,0:T(8,128)(2,1)} async-done(((bf16[2048,512]{1,0:T(8,128)(2,1)}), bf16[4096,512]{1,0:T(8,128)(2,1)}) %all-gather.7.cloned.1.call-update) | async-done | bytes 4194320 | tf_op jit(solution)/shard_map/all_gather | solution.py:52
  70.3 2.9 fusion.19
  73.2 0.2 reshape.159
  73.4 0.1 slice.30
  73.5 0.1 slice.27
  73.7 0.1 slice_negate_fusion.1
  73.8 0.1 fusion.25
  73.9 0.7 pad_maximum_fusion
  74.6 0.0 all-gather.9.cloned.1.call-update
  74.6 0.0 all-gather.11.cloned.1.call-start
  74.7 0.5 all-gather.11.cloned.1.call-update
  75.2 0.0 reduce-scatter.2.cloned.1.call-start
  75.2 0.1 select_reduce_fusion
  75.4 0.4 broadcast_compare_fusion
  75.7 100.1 %all-gather.5.cloned.1.call-done = bf16[4096,1024]{1,0:T(8,128)(2,1)} async-done(((bf16[2048,1024]{1,0:T(8,128)(2,1)}), bf16[4096,1024]{1,0:T(8,128)(2,1)}) %all-gather.5.cloned.1.call-update) | async-done | bytes 8388624 | tf_op jit(solution)/shard_map/all_gather | solution.py:47
  175.9 4.7 %fusion.21 = f32[128,1024]{1,0:T(8,128)S(1)} fusion(bf16[4096,1024]{1,0:T(8,128)(2,1)} %all-gather.5.cloned.1.call-done, bf16[128,4096]{1,0:T(8,128)(2,1)S(1)} %copy-done, f32[128]{0:T(128)S(1)} %add_rsqrt_fusion), kind=kOutput, calls=%fused_computation.23 | convolution fusion | flops 1075314688 | bytes 9961984 | tf_op jit(solution)/shard_map/dot_general | solution.py:45
  180.5 0.2 reshape.155
  180.8 0.1 copy.19
  180.9 0.2 slice_negate_fusion
  181.1 0.4 fusion.23
  181.6 36.7 %all-gather.9.cloned.1.call-done = bf16[1024,4,128]{2,0,1:T(8,128)(2,1)} async-done(((bf16[128,4,128]{2,0,1:T(8,128)(2,1)}), bf16[1024,4,128]{2,0,1:T(8,128)(2,1)}) %all-gather.9.cloned.1.call-update) | async-done | bytes 1048592 | tf_op jit(solution)/shard_map/all_gather | solution.py:65
  218.3 0.0 copy-start.2
  218.3 2.2 fusion
  220.5 1.5 fusion.1
  221.9 0.0 copy-done.2
  221.9 1.1 fusion.11
  223.0 0.2 copy.16
  223.2 99.3 %all-gather.11.cloned.1.call-done = bf16[1024,4096]{1,0:T(8,128)(2,1)} async-done(((bf16[1024,2048]{1,0:T(8,128)(2,1)}), bf16[1024,4096]{1,0:T(8,128)(2,1)}) %all-gather.11.cloned.1.call-update) | async-done | bytes 8388624 | tf_op jit(solution)/shard_map/all_gather | solution.py:92
  322.5 5.6 %convolution_convert_fusion = bf16[128,4096]{1,0:T(8,128)(2,1)} fusion(bf16[128,1024]{0,1:T(8,128)(2,1)S(1)} %bitcast.30, bf16[1024,4096]{1,0:T(8,128)(2,1)} %all-gather.11.cloned.1.call-done), kind=kOutput, calls=%fused_computation | convolution fusion | flops 1074266112 | bytes 9699328 | tf_op jit(solution)/shard_map/dot_general | solution.py:90
  328.1 0.0 reduce-scatter.2.cloned.1.call-update
  328.1 8.7 %reduce-scatter.2.cloned.1.call-done = bf16[128,2048]{1,0:T(8,128)(2,1)} async-done(((bf16[128,4096]{1,0:T(8,128)(2,1)}), bf16[128,2048]{1,0:T(8,128)(2,1)}) %reduce-scatter.2.cloned.1.call-update) | async-done | bytes 524304 | tf_op jit(solution)/shard_map/reduce_scatter | solution.py:95
  (11 shorter events, 0.1 us)
Async XLA Ops:
  6.5 63.7 %all-gather.7.cloned.1.call-start = ((), (), s32[]{:S(2)}) async-start(), calls=%async_computation.2 | async-start | bytes 6291456 | tf_op jit(solution)/shard_map/all_gather | solution.py:52
  10.6 0.9 copy-start.1
  10.6 1.4 copy-start
  10.7 165.2 %all-gather.5.cloned.1.call-start = ((), (), s32[]{:S(2)}) async-start(), calls=%async_computation.1 | async-start | bytes 12582912 | tf_op jit(solution)/shard_map/all_gather | solution.py:47
  11.4 206.9 %all-gather.9.cloned.1.call-start = ((), (), s32[]{:S(2)}) async-start(), calls=%async_computation.3 | async-start | bytes 1179648 | tf_op jit(solution)/shard_map/all_gather | solution.py:65
  74.6 247.9 %all-gather.11.cloned.1.call-start = ((), (), s32[]{:S(2)}) async-start(), calls=%async_computation.4 | async-start | bytes 12582912 | tf_op jit(solution)/shard_map/all_gather | solution.py:92
  75.2 261.7 %reduce-scatter.2.cloned.1.call-start = ((), (), s32[]{:S(2)}) async-start(), calls=%async_computation.5 | async-start | bytes 1572864 | tf_op jit(solution)/shard_map/reduce_scatter | solution.py:95
  218.3 3.7 %copy-start.2 = (bf16[1024,4,128]{2,0,1:T(8,128)(2,1)S(1)}, bf16[1024,4,128]{2,0,1:T(8,128)(2,1)}, u32[]{:S(2)}) copy-start(bf16[1024,4,128]{2,0,1:T(8,128)(2,1)} %all-gather.9.cloned.1.call-done) | copy-start | bytes 3145732
Sparse Core Ops, SparseCore 0:
  10.8 59.4 all-gather.6
  71.8 103.9 all-gather.4
  178.0 40.1 all-gather.8
  219.7 102.7 all-gather.10
  328.2 8.5 reduce-scatter.1
